TPU v7x, 128 devices: a whole 4x4x4 slice. The times are simulated.
128 devices in a mesh: pts: 16 (over y, z), var: 8 (over x, core).
Axes of the slice: x: 4, y: 4, z: 4, core: 2. Of those that a mesh axis runs over, the one named last changes fastest.
Arguments:
- tensor: bfloat16 [8, 16384, 8192], P(None, 'pts', 'var'), may hold values from -36 to 36
- level_init: float32 [64, 8192], P(None, 'var'), may hold values from -6 to 6
- time_init: float32 [8, 64], replicated, may hold values from -6 to 6
Outputs:
- point_factor: float32 [64, 16384], P(None, 'pts')
- level_factor: float32 [64, 8192], P(None, 'var')
- time_out: float32 [8, 64], replicated
All inputs are finite; a program needn't handle non-finite values.
Results may differ from a plain program's by a relative error of at most 0.011.
Values sent between devices are 32-bit elements; how exact they have to be, the bound alone decides.
A program may use at most 128 MiB of HBM per device.

v0:
```python
import math

import jax
import jax.numpy as jnp
from jax import lax
from jax.sharding import Mesh
from jax.sharding import PartitionSpec as P

STEPS = 8
SWEEPS = 3
VAR = ("var_0", "var_1")
PTS = ("pts_0", "pts_1")


HIGH_PRECISION = lax.Precision.HIGHEST
EPSILON = 1e-06


def total_of_pieces(array, axis):
    return lax.all_gather(array, axis).sum(0)


def copy_for_each(array, axis):
    devices = lax.axis_size(axis)
    return lax.all_to_all(
        jnp.broadcast_to(array[None], (devices, *array.shape)), axis, 0, 0, tiled=True
    )


def over_copies(array, axis):
    everything = copy_for_each(array, axis)
    return jnp.sum(everything, axis=0)


def by_axis(array, axes):
    far, near = axes
    return over_copies(over_copies(array, near), far)


def split_up(array, dim, devices):
    shape = array.shape
    pieces = array.reshape(*shape[:dim], devices, shape[dim] // devices, *shape[dim + 1 :])
    return jnp.moveaxis(pieces, dim, 0)


def sent_and_summed(array, axis, dim):
    devices = lax.axis_size(axis)
    pieces = lax.all_to_all(split_up(array, dim, devices), axis, 0, 0, tiled=True)
    return jnp.sum(pieces, axis=0)


def rows_for(lines, devices):
    spare = -lines.shape[0] % devices
    if not spare:
        return lines
    return jnp.concatenate([lines, jnp.zeros((spare, *lines.shape[1:]), lines.dtype)])


def joined_along(pieces, dim):
    shape = list(pieces.shape[1:])
    shape[dim] *= pieces.shape[0]
    return jnp.moveaxis(pieces, 0, dim).reshape(shape)


def gather_directly(array, axis, dim):
    return joined_along(copy_for_each(array, axis), dim)


def sum_by_parts(array, axes):
    lines = array.reshape(-1, array.shape[-1])
    own = sent_and_summed(rows_for(lines, lax.axis_size(axes)), axes, 0)
    whole = gather_directly(own, axes, 0)
    return whole[: len(lines)].reshape(array.shape)


def gram_of(factor):
    return jnp.dot(factor, factor.T, precision=HIGH_PRECISION, preferred_element_type=jnp.float32)


def ridge_solve(gram_mat, right_side):
    order_count = gram_mat.shape[0]
    ridge_term = 0.01 * jnp.trace(gram_mat) / order_count + EPSILON
    system = gram_mat + ridge_term * jnp.eye(order_count, dtype=jnp.float32)
    chol_lower = jnp.linalg.cholesky(system)
    middle = lax.linalg.triangular_solve(chol_lower, right_side, left_side=True, lower=True)
    return lax.linalg.triangular_solve(
        chol_lower, middle, left_side=True, lower=True, transpose_a=True
    )


def time_products(stacked, factor):
    return jnp.sum(stacked * factor[None, :, :], axis=2)


def update_points(mttk_point, system_gram, points_all):
    share_width = mttk_point.shape[1] // lax.axis_size(VAR)
    summed = total_of_pieces(mttk_point, VAR)
    solved = ridge_solve(system_gram, summed)
    share_cols = lax.dynamic_slice_in_dim(solved, lax.axis_index(VAR) * share_width, share_width, 1)
    whole_gram = by_axis(gram_of(share_cols), (("pts_0", "pts_1"), ("var_0", "var_1")))
    col_scale = 1.0 / jnp.sqrt(jnp.diagonal(whole_gram) / points_all + EPSILON)
    new_gram = col_scale[:, None] * whole_gram * col_scale[None, :]
    return (solved * col_scale[:, None], new_gram)


def update_levels(mttk_level, stacked, system_gram, levels_all):
    share_width = mttk_level.shape[1] // lax.axis_size(PTS)
    share_start = lax.axis_index(PTS) * share_width
    summed = sum_by_parts(mttk_level, PTS)
    solved = ridge_solve(system_gram, summed)
    share_cols = lax.dynamic_slice_in_dim(solved, share_start, share_width, 1)
    raw_time = time_products(stacked, solved)
    whole_gram, time_sum = (
        by_axis(gram_of(share_cols), (("pts_0", "pts_1"), ("var_0", "var_1"))),
        by_axis(raw_time, (("pts_0", "pts_1"), ("var_0", "var_1"))),
    )
    col_scale = 1.0 / jnp.sqrt(jnp.diagonal(whole_gram) / levels_all + EPSILON)
    new_gram = col_scale[:, None] * whole_gram * col_scale[None, :]
    mttk_time = time_sum * col_scale[None, :]
    return (solved * col_scale[:, None], new_gram, mttk_time)


def per_device(tensor, level_init, time_init):
    points_all = tensor.shape[1] * lax.axis_size(PTS)
    levels_all = tensor.shape[2] * lax.axis_size(VAR)
    level_factor = level_init
    level_grammat = over_copies(gram_of(level_init), VAR)
    time_factor = time_init
    point_factor = None
    for sweep_index in range(SWEEPS):
        time_gram = jnp.dot(
            time_factor.T, time_factor, precision=HIGH_PRECISION, preferred_element_type=jnp.float32
        )
        level_bf = level_factor.astype(jnp.bfloat16)
        mttk_point = jnp.zeros((level_factor.shape[0], tensor.shape[1]), jnp.float32)
        for step_index in range(STEPS):
            product = jnp.einsum(
                "rv,pv->rp", level_bf, tensor[step_index], preferred_element_type=jnp.float32
            )
            mttk_point = mttk_point + time_factor[step_index][:, None] * product
        point_factor, point_grammat = update_points(
            mttk_point, level_grammat * time_gram, points_all
        )
        point_bf = point_factor.astype(jnp.bfloat16)
        mttk_level = jnp.zeros((point_factor.shape[0], tensor.shape[2]), jnp.float32)
        contracted = []
        for step_index in range(STEPS):
            product = jnp.dot(point_bf, tensor[step_index], preferred_element_type=jnp.float32)
            contracted.append(product)
            mttk_level = mttk_level + time_factor[step_index][:, None] * product
        stacked = jnp.stack(contracted)
        level_factor, level_grammat, mttk_time = update_levels(
            mttk_level, stacked, point_grammat * time_gram, levels_all
        )
        time_factor = ridge_solve(point_grammat * level_grammat, mttk_time.T).T
    return (point_factor, level_factor, time_factor * math.sqrt(points_all * levels_all))


def solution(mesh):
    torus = Mesh(mesh.devices.reshape(4, 4, 4, 2), ("pts_0", "pts_1", "var_0", "var_1"))
    return jax.shard_map(
        per_device,
        mesh=torus,
        in_specs=(P(None, PTS, VAR), P(None, VAR), P()),
        out_specs=(P(None, PTS), P(None, VAR), P()),
        check_vma=False,
    )
```

profile of v0, /device:TPU:0, one launch (start us, length us, event | category | flops | bytes accessed | tf_op | source)
XLA Modules:
  0.0 563.0 jit_solution(2541950905098205122)
XLA Ops:
  34.4 6.1 %all-to-all-done = f32[8,1,4096]{2,1,0:T(1,128)S(1)} async-done(((f32[8,1,4096]{2,1,0:T(1,128)}), f32[8,1,4096]{2,1,0:T(1,128)S(1)}, u32[]{:S(2)}, u32[]{:S(2)}) %all-to-all-start) | async-done | bytes 131104 | tf_op jit(solution)/shard_map/all_to_all | solution.py:25
  43.9 5.8 %cholesky.149 = f32[64,64]{1,0:T(8,128)S(1)} custom-call(f32[64,64]{1,0:T(8,128)S(1)} %fusion.332), custom_call_target="Cholesky" | custom-call | tf_op jit(solution)/shard_map/jit(cholesky)/cholesky | solution.py:84
  59.7 9.1 %all_to_all.125 = f32[8,1,4096]{2,1,0:T(1,128)S(1)} all-to-all(f32[8,1,4096]{2,1,0:T(1,128)S(1)} %reshape.273), channel_id=1, replica_groups=mesh['pts_0'=4,'pts_1'=4,'var_0'=4,'var_1'=2] {'var_0','var_1'}, dimensions={0} | all-to-all | bytes 262144 | tf_op jit(solution)/shard_map/all_to_all | solution.py:25
  70.9 7.3 %all-to-all-start.2 = ((f32[16,1,4096]{2,1,0:T(1,128)}), f32[16,1,4096]{2,1,0:T(1,128)S(1)}, u32[]{:S(2)}, u32[]{:S(2)}) async-start(f32[16,1,4096]{2,1,0:T(1,128)} %reshape.275), calls=%async_computation.2 | async-start | bytes 524288 | tf_op jit(solution)/shard_map/all_to_all | solution.py:25
  78.3 8.5 %all-to-all-done.2 = f32[16,1,4096]{2,1,0:T(1,128)S(1)} async-done(((f32[16,1,4096]{2,1,0:T(1,128)}), f32[16,1,4096]{2,1,0:T(1,128)S(1)}, u32[]{:S(2)}, u32[]{:S(2)}) %all-to-all-start.2) | async-done | bytes 262176 | tf_op jit(solution)/shard_map/all_to_all | solution.py:25
  112.1 5.8 %cholesky.160 = f32[64,64]{1,0:T(8,128)S(1)} custom-call(f32[64,64]{1,0:T(8,128)S(1)} %fusion.327), custom_call_target="Cholesky" | custom-call | tf_op jit(solution)/shard_map/jit(cholesky)/cholesky | solution.py:84
  121.3 5.3 all-to-all-start.4
  161.5 5.4 all-to-all-done.8
  171.8 7.2 %all-to-all-done.6 = f32[16,1,4096]{2,1,0:T(1,128)S(1)} async-done(((f32[16,1,4096]{2,1,0:T(1,128)}), f32[16,1,4096]{2,1,0:T(1,128)S(1)}, u32[]{:S(2)}, u32[]{:S(2)}) %all-to-all-start.6) | async-done | bytes 262176 | tf_op jit(solution)/shard_map/all_to_all | solution.py:25
  183.0 5.8 %cholesky.171 = f32[64,64]{1,0:T(8,128)S(1)} custom-call(f32[64,64]{1,0:T(8,128)S(1)} %fusion.322), custom_call_target="Cholesky" | custom-call | tf_op jit(solution)/shard_map/jit(cholesky)/cholesky | solution.py:84
  190.2 4.9 custom-call.45
  216.7 5.8 %cholesky.182 = f32[64,64]{1,0:T(8,128)S(1)} custom-call(f32[64,64]{1,0:T(8,128)S(1)} %fusion.317), custom_call_target="Cholesky" | custom-call | tf_op jit(solution)/shard_map/jit(cholesky)/cholesky | solution.py:84
  223.9 4.9 custom-call.47
  228.8 8.0 %all-gather.9.cloned.1.call-done = f32[512,1024]{1,0:T(8,128)} async-done(((f32[64,1024]{1,0:T(8,128)}), f32[512,1024]{1,0:T(8,128)}) %all-gather.9.cloned.1.call-update) | async-done | bytes 2097168 | tf_op jit(solution)/shard_map/all_gather | solution.py:20
  239.7 9.0 %all_to_all.126 = f32[8,1,4096]{2,1,0:T(1,128)S(1)} all-to-all(f32[8,1,4096]{2,1,0:T(1,128)S(1)} %reshape.285), channel_id=1, replica_groups=mesh['pts_0'=4,'pts_1'=4,'var_0'=4,'var_1'=2] {'var_0','var_1'}, dimensions={0} | all-to-all | bytes 262144 | tf_op jit(solution)/shard_map/all_to_all | solution.py:25
  250.2 15.6 %all_to_all.127 = f32[16,1,4096]{2,1,0:T(1,128)S(1)} all-to-all(f32[16,1,4096]{2,1,0:T(1,128)S(1)} %reshape.287), channel_id=1, replica_groups=mesh['pts_0'=4,'pts_1'=4,'var_0'=4,'var_1'=2] {'pts_0','pts_1'}, dimensions={0} | all-to-all | bytes 524288 | tf_op jit(solution)/shard_map/all_to_all | solution.py:25
  291.1 5.8 %cholesky.193 = f32[64,64]{1,0:T(8,128)S(1)} custom-call(f32[64,64]{1,0:T(8,128)S(1)} %fusion.312), custom_call_target="Cholesky" | custom-call | tf_op jit(solution)/shard_map/jit(cholesky)/cholesky | solution.py:84
  300.4 5.3 all-to-all-start.12
  340.6 5.4 all-to-all-done.16
  350.6 7.3 %all-to-all-done.14 = f32[16,1,4096]{2,1,0:T(1,128)S(1)} async-done(((f32[16,1,4096]{2,1,0:T(1,128)}), f32[16,1,4096]{2,1,0:T(1,128)S(1)}, u32[]{:S(2)}, u32[]{:S(2)}) %all-to-all-start.14) | async-done | bytes 262176 | tf_op jit(solution)/shard_map/all_to_all | solution.py:25
  362.1 5.8 %cholesky.204 = f32[64,64]{1,0:T(8,128)S(1)} custom-call(f32[64,64]{1,0:T(8,128)S(1)} %fusion.307), custom_call_target="Cholesky" | custom-call | tf_op jit(solution)/shard_map/jit(cholesky)/cholesky | solution.py:84
  395.8 5.8 %cholesky.215 = f32[64,64]{1,0:T(8,128)S(1)} custom-call(f32[64,64]{1,0:T(8,128)S(1)} %fusion.302), custom_call_target="Cholesky" | custom-call | tf_op jit(solution)/shard_map/jit(cholesky)/cholesky | solution.py:84
  403.0 4.9 custom-call.53
  407.9 8.0 %all-gather.11.cloned.1.call-done = f32[512,1024]{1,0:T(8,128)} async-done(((f32[64,1024]{1,0:T(8,128)}), f32[512,1024]{1,0:T(8,128)}) %all-gather.11.cloned.1.call-update) | async-done | bytes 2097168 | tf_op jit(solution)/shard_map/all_gather | solution.py:20
  418.8 9.0 %all_to_all.128 = f32[8,1,4096]{2,1,0:T(1,128)S(1)} all-to-all(f32[8,1,4096]{2,1,0:T(1,128)S(1)} %reshape.297), channel_id=1, replica_groups=mesh['pts_0'=4,'pts_1'=4,'var_0'=4,'var_1'=2] {'var_0','var_1'}, dimensions={0} | all-to-all | bytes 262144 | tf_op jit(solution)/shard_map/all_to_all | solution.py:25
  429.3 15.7 %all_to_all.129 = f32[16,1,4096]{2,1,0:T(1,128)S(1)} all-to-all(f32[16,1,4096]{2,1,0:T(1,128)S(1)} %reshape.299), channel_id=1, replica_groups=mesh['pts_0'=4,'pts_1'=4,'var_0'=4,'var_1'=2] {'pts_0','pts_1'}, dimensions={0} | all-to-all | bytes 524288 | tf_op jit(solution)/shard_map/all_to_all | solution.py:25
  471.0 5.8 %cholesky.226 = f32[64,64]{1,0:T(8,128)S(1)} custom-call(f32[64,64]{1,0:T(8,128)S(1)} %fusion.297), custom_call_target="Cholesky" | custom-call | tf_op jit(solution)/shard_map/jit(cholesky)/cholesky | solution.py:84
  480.2 5.4 all-to-all-start.20
  520.5 5.4 all-to-all-done.24
  530.6 7.6 %all-to-all-done.22 = f32[16,1,4096]{2,1,0:T(1,128)S(1)} async-done(((f32[16,1,4096]{2,1,0:T(1,128)}), f32[16,1,4096]{2,1,0:T(1,128)S(1)}, u32[]{:S(2)}, u32[]{:S(2)}) %all-to-all-start.22) | async-done | bytes 262176 | tf_op jit(solution)/shard_map/all_to_all | solution.py:25
  543.0 5.8 %cholesky.237 = f32[64,64]{1,0:T(8,128)S(1)} custom-call(f32[64,64]{1,0:T(8,128)S(1)} %fusion.292), custom_call_target="Cholesky" | custom-call | tf_op jit(solution)/shard_map/jit(cholesky)/cholesky | solution.py:84
  550.2 4.9 custom-call.57
  (327 shorter events, 318.8 us)
Async XLA Ops:
  7.2 49.6 %all-gather.7.cloned.1.call-start = ((), (), s32[]{:S(2)}) async-start(), calls=%async_computation.25 | async-start | bytes 2359296 | tf_op jit(solution)/shard_map/all_gather | solution.py:20
  25.7 3.2 copy-start
  25.7 16.6 %copy-start.1 = (f32[8,64]{1,0:T(8,128)S(1)}, f32[8,64]{1,0:T(8,128)}, u32[]{:S(2)}) copy-start(f32[8,64]{1,0:T(8,128)} %param.14) | copy-start | bytes 6148
  30.0 10.5 %all-to-all-start = ((f32[8,1,4096]{2,1,0:T(1,128)}), f32[8,1,4096]{2,1,0:T(1,128)S(1)}, u32[]{:S(2)}, u32[]{:S(2)}) async-start(f32[8,1,4096]{2,1,0:T(1,128)} %reshape.271), calls=%async_computation | async-start | bytes 262144 | tf_op jit(solution)/shard_map/all_to_all | solution.py:25
  70.9 15.8 %all-to-all-start.2 = ((f32[16,1,4096]{2,1,0:T(1,128)}), f32[16,1,4096]{2,1,0:T(1,128)S(1)}, u32[]{:S(2)}, u32[]{:S(2)}) async-start(f32[16,1,4096]{2,1,0:T(1,128)} %reshape.275), calls=%async_computation.2 | async-start | bytes 524288 | tf_op jit(solution)/shard_map/all_to_all | solution.py:25
  108.4 12.1 %all-to-all-start.3 = ((f32[16,4,1024]{2,1,0:T(4,128)}), f32[16,4,1024]{2,1,0:T(4,128)S(1)}, u32[]{:S(2)}, u32[]{:S(2)}) async-start(f32[16,4,1024]{2,1,0:T(4,128)} %reshape.162), calls=%async_computation.3 | async-start | bytes 524288 | tf_op jit(solution)/shard_map/all_to_all | solution.py:48
  121.3 13.8 %all-to-all-start.4 = ((f32[16,4,1024]{2,1,0:T(4,128)}), f32[16,4,1024]{2,1,0:T(4,128)S(1)}, u32[]{:S(2)}, u32[]{:S(2)}) async-start(f32[16,4,1024]{2,1,0:T(4,128)} %broadcast_in_dim.75), calls=%async_computation.4 | async-start | bytes 524288 | tf_op jit(solution)/shard_map/all_to_all | solution.py:25
  136.9 8.6 %all-to-all-start.7 = ((f32[8,1,512]{2,1,0:T(1,128)}), f32[8,1,512]{2,1,0:T(1,128)S(1)}, u32[]{:S(2)}, u32[]{:S(2)}) async-start(f32[8,1,512]{2,1,0:T(1,128)} %reshape.281), calls=%async_computation.7 | async-start | bytes 32768 | tf_op jit(solution)/shard_map/all_to_all | solution.py:25
  145.5 9.4 %all-to-all-start.5 = ((f32[8,1,4096]{2,1,0:T(1,128)}), f32[8,1,4096]{2,1,0:T(1,128)S(1)}, u32[]{:S(2)}, u32[]{:S(2)}) async-start(f32[8,1,4096]{2,1,0:T(1,128)} %reshape.277), calls=%async_computation.5 | async-start | bytes 262144 | tf_op jit(solution)/shard_map/all_to_all | solution.py:25
  155.0 12.0 %all-to-all-start.8 = ((f32[16,1,512]{2,1,0:T(1,128)}), f32[16,1,512]{2,1,0:T(1,128)S(1)}, u32[]{:S(2)}, u32[]{:S(2)}) async-start(f32[16,1,512]{2,1,0:T(1,128)} %reshape.283), calls=%async_computation.8 | async-start | bytes 65536 | tf_op jit(solution)/shard_map/all_to_all | solution.py:25
  166.9 12.0 %all-to-all-start.6 = ((f32[16,1,4096]{2,1,0:T(1,128)}), f32[16,1,4096]{2,1,0:T(1,128)S(1)}, u32[]{:S(2)}, u32[]{:S(2)}) async-start(f32[16,1,4096]{2,1,0:T(1,128)} %reshape.279), calls=%async_computation.6 | async-start | bytes 524288 | tf_op jit(solution)/shard_map/all_to_all | solution.py:25
  170.5 66.3 %all-gather.9.cloned.1.call-start = ((), (), s32[]{:S(2)}) async-start(), calls=%async_computation.26 | async-start | bytes 2359296 | tf_op jit(solution)/shard_map/all_gather | solution.py:20
  287.5 12.1 %all-to-all-start.11 = ((f32[16,4,1024]{2,1,0:T(4,128)}), f32[16,4,1024]{2,1,0:T(4,128)S(1)}, u32[]{:S(2)}, u32[]{:S(2)}) async-start(f32[16,4,1024]{2,1,0:T(4,128)} %reshape.164), calls=%async_computation.11 | async-start | bytes 524288 | tf_op jit(solution)/shard_map/all_to_all | solution.py:48
  300.4 13.8 %all-to-all-start.12 = ((f32[16,4,1024]{2,1,0:T(4,128)}), f32[16,4,1024]{2,1,0:T(4,128)S(1)}, u32[]{:S(2)}, u32[]{:S(2)}) async-start(f32[16,4,1024]{2,1,0:T(4,128)} %broadcast_in_dim.82), calls=%async_computation.12 | async-start | bytes 524288 | tf_op jit(solution)/shard_map/all_to_all | solution.py:25
  316.0 8.6 %all-to-all-start.15 = ((f32[8,1,512]{2,1,0:T(1,128)}), f32[8,1,512]{2,1,0:T(1,128)S(1)}, u32[]{:S(2)}, u32[]{:S(2)}) async-start(f32[8,1,512]{2,1,0:T(1,128)} %reshape.293), calls=%async_computation.15 | async-start | bytes 32768 | tf_op jit(solution)/shard_map/all_to_all | solution.py:25
  324.6 9.4 %all-to-all-start.13 = ((f32[8,1,4096]{2,1,0:T(1,128)}), f32[8,1,4096]{2,1,0:T(1,128)S(1)}, u32[]{:S(2)}, u32[]{:S(2)}) async-start(f32[8,1,4096]{2,1,0:T(1,128)} %reshape.289), calls=%async_computation.13 | async-start | bytes 262144 | tf_op jit(solution)/shard_map/all_to_all | solution.py:25
  334.0 12.0 %all-to-all-start.16 = ((f32[16,1,512]{2,1,0:T(1,128)}), f32[16,1,512]{2,1,0:T(1,128)S(1)}, u32[]{:S(2)}, u32[]{:S(2)}) async-start(f32[16,1,512]{2,1,0:T(1,128)} %reshape.295), calls=%async_computation.16 | async-start | bytes 65536 | tf_op jit(solution)/shard_map/all_to_all | solution.py:25
  346.0 12.0 %all-to-all-start.14 = ((f32[16,1,4096]{2,1,0:T(1,128)}), f32[16,1,4096]{2,1,0:T(1,128)S(1)}, u32[]{:S(2)}, u32[]{:S(2)}) async-start(f32[16,1,4096]{2,1,0:T(1,128)} %reshape.291), calls=%async_computation.14 | async-start | bytes 524288 | tf_op jit(solution)/shard_map/all_to_all | solution.py:25
  349.6 66.3 %all-gather.11.cloned.1.call-start = ((), (), s32[]{:S(2)}) async-start(), calls=%async_computation.27 | async-start | bytes 2359296 | tf_op jit(solution)/shard_map/all_gather | solution.py:20
  467.3 12.1 %all-to-all-start.19 = ((f32[16,4,1024]{2,1,0:T(4,128)}), f32[16,4,1024]{2,1,0:T(4,128)S(1)}, u32[]{:S(2)}, u32[]{:S(2)}) async-start(f32[16,4,1024]{2,1,0:T(4,128)} %reshape.166), calls=%async_computation.19 | async-start | bytes 524288 | tf_op jit(solution)/shard_map/all_to_all | solution.py:48
  480.2 13.8 %all-to-all-start.20 = ((f32[16,4,1024]{2,1,0:T(4,128)}), f32[16,4,1024]{2,1,0:T(4,128)S(1)}, u32[]{:S(2)}, u32[]{:S(2)}) async-start(f32[16,4,1024]{2,1,0:T(4,128)} %broadcast_in_dim.89), calls=%async_computation.20 | async-start | bytes 524288 | tf_op jit(solution)/shard_map/all_to_all | solution.py:25
  495.9 8.6 %all-to-all-start.23 = ((f32[8,1,512]{2,1,0:T(1,128)}), f32[8,1,512]{2,1,0:T(1,128)S(1)}, u32[]{:S(2)}, u32[]{:S(2)}) async-start(f32[8,1,512]{2,1,0:T(1,128)} %reshape.305), calls=%async_computation.23 | async-start | bytes 32768 | tf_op jit(solution)/shard_map/all_to_all | solution.py:25
  504.5 9.4 %all-to-all-start.21 = ((f32[8,1,4096]{2,1,0:T(1,128)}), f32[8,1,4096]{2,1,0:T(1,128)S(1)}, u32[]{:S(2)}, u32[]{:S(2)}) async-start(f32[8,1,4096]{2,1,0:T(1,128)} %reshape.301), calls=%async_computation.21 | async-start | bytes 262144 | tf_op jit(solution)/shard_map/all_to_all | solution.py:25
  513.9 12.0 %all-to-all-start.24 = ((f32[16,1,512]{2,1,0:T(1,128)}), f32[16,1,512]{2,1,0:T(1,128)S(1)}, u32[]{:S(2)}, u32[]{:S(2)}) async-start(f32[16,1,512]{2,1,0:T(1,128)} %reshape.307), calls=%async_computation.24 | async-start | bytes 65536 | tf_op jit(solution)/shard_map/all_to_all | solution.py:25
  526.0 12.3 %all-to-all-start.22 = ((f32[16,1,4096]{2,1,0:T(1,128)}), f32[16,1,4096]{2,1,0:T(1,128)S(1)}, u32[]{:S(2)}, u32[]{:S(2)}) async-start(f32[16,1,4096]{2,1,0:T(1,128)} %reshape.303), calls=%async_computation.22 | async-start | bytes 524288 | tf_op jit(solution)/shard_map/all_to_all | solution.py:25
Sparse Core Ops, SparseCore 0:
  28.9 27.7 all-gather.6
  215.2 21.5 all-gather.8
  394.2 21.5 all-gather.10
where the time goes:
time: 574 us; the launch traced here: 563 us
  other arithmetic  142 us (25%)
  matrix products  120 us (21%)
  waiting for transfers between devices  110 us (19%)
  starting transfers between devices  83.4 us (15%)
  blocking collectives  58.4 us (10%)
  local copies, waits for them, and re-layouts  28.3 us (5%)
  between operations  21.5 us (4%)
    all_to_all x17, waiting for transfers between devices, copy_for_each(): lax.all_to_all(jnp.broadcast_to(array[None], (devices, *array.shape)), ax...  87.7 us
    all_to_all x17, starting transfers between devices, copy_for_each(): lax.all_to_all(jnp.broadcast_to(array[None], (devices, *array.shape)), ax...  71.7 us
    dot_general x24, matrix products, per_device(): jnp.einsum('rv,pv->rp', level_bf, tensor[step_index], preferred_element_t...  58.8 us
    another operation x27, other arithmetic, ridge_solve(): chol_lower = jnp.linalg.cholesky(system)  58.7 us
    all_to_all x5, blocking collectives, copy_for_each(): lax.all_to_all(jnp.broadcast_to(array[None], (devices, *array.shape)), ax...  58.4 us
    dot_general x24, matrix products, per_device(): jnp.dot(point_bf, tensor[step_index], preferred_element_type=jnp.float32)  50.3 us
    another operation x18, other arithmetic, ridge_solve(): lax.linalg.triangular_solve(chol_lower, middle, left_side=True, lower=Tru...  50 us
    all_to_all x19, other arithmetic, copy_for_each(): lax.all_to_all(jnp.broadcast_to(array[None], (devices, *array.shape)), ax...  18.6 us
  transfers between devices with their start and end apart: 23, of which 23 were waited for; matrix products, arithmetic and copies ran while one was open for 17% of the time, Pallas kernels for 0%

commit v1 on v0

v1 whole, which is shorter than its diff:
```python
import math

import jax
import jax.numpy as jnp
from jax import lax
from jax.experimental import pallas as pl
from jax.experimental.pallas import tpu as pltpu
from jax.sharding import PartitionSpec as P

RANK = 64
STEPS = 8
SWEEPS = 3
NY = NZ = NX = 4
PTS_DEVICES = NY * NZ
CHIPS = PTS_DEVICES * NX
EPSILON = 1e-06
F32 = jnp.float32
BF16 = jnp.bfloat16
HIGHEST = lax.Precision.HIGHEST
MESH = pl.DeviceIdType.MESH


def spd_inverse(matrix, block=8):
    n = RANK
    shape = (8, n)
    row_ids = lax.broadcasted_iota(jnp.int32, shape, 0)
    lane_ids = lax.broadcasted_iota(jnp.int32, shape, 1)
    tiles = [matrix[8 * i : 8 * i + 8, :] for i in range(n // 8)]
    for start in range(0, n, block):
        panel = {
            j: [jnp.broadcast_to(tile[:, j : j + 1], shape) for tile in tiles]
            for j in range(start, start + block)
        }
        for k in range(start, start + block):
            t, s = divmod(k, 8)
            inv_pivot = 1.0 / jnp.broadcast_to(panel[k][t][s : s + 1, :], shape)
            col = list(panel[k])
            col[t] = jnp.where(row_ids == s, -1.0, col[t])
            for j in range(k + 1, start + block):
                scaled = jnp.broadcast_to(panel[j][t][s : s + 1, :], shape) * inv_pivot
                new = [panel[j][i] - col[i] * scaled for i in range(n // 8)]
                new[t] = jnp.where(row_ids == s, scaled, new[t])
                panel[j] = new
            row = jnp.broadcast_to(tiles[t][s : s + 1, :], shape) * inv_pivot
            row = jnp.where(lane_ids == k, inv_pivot, row)
            base = [jnp.where(lane_ids == k, 0.0, tile) for tile in tiles]
            base[t] = jnp.where(row_ids == s, 0.0, base[t])
            tiles = [base[i] - col[i] * row for i in range(n // 8)]
    return jnp.concatenate(tiles, axis=0)


def eye_mask():
    rows = lax.broadcasted_iota(jnp.int32, (RANK, RANK), 0)
    cols = lax.broadcasted_iota(jnp.int32, (RANK, RANK), 1)
    return rows == cols


def ridge_inverse(gram):
    eye = eye_mask()
    trace = jnp.sum(
        jnp.sum(jnp.where(eye, gram, 0.0), axis=0, keepdims=True), axis=1, keepdims=True
    )
    ridge = 0.01 * trace / RANK + EPSILON
    return spd_inverse(gram + jnp.where(eye, ridge, 0.0))


def packed_gram(factor):
    high = factor.astype(BF16)
    low = (factor - high.astype(F32)).astype(BF16)
    both = jnp.concatenate([high, low], axis=0)
    g = lax.dot_general(both, both, (((1,), (1,)), ((), ())), preferred_element_type=F32)
    rows = g[:RANK] + g[RANK:]
    gram = rows[:, :RANK] + rows[:, RANK:]
    return jnp.concatenate([gram[:32], gram[32:]], axis=1)


def unpacked(folded):
    return jnp.concatenate([folded[:, :RANK], folded[:, RANK:]], axis=0)


def unit_scales(gram, count):
    diag = jnp.where(eye_mask(), gram, 0.0)
    col = 1.0 / jnp.sqrt(jnp.sum(diag, axis=1, keepdims=True) / count + EPSILON)
    row = 1.0 / jnp.sqrt(jnp.sum(diag, axis=0, keepdims=True) / count + EPSILON)
    return col, row


def sweeps_kernel(
    points_all,
    levels_all,
    x_hbm,
    level_ref,
    time_ref,
    point_out,
    level_out,
    time_out,
    x_ref,
    y_ref,
    c_ref,
    lbf_ref,
    pbf_ref,
    lu_ref,
    pu_ref,
    gl_ref,
    gp_ref,
    tt_ref,
    tr_ref,
    slcol_ref,
    mp_ref,
    sib_mp,
    rs_mp,
    m_full,
    g_send,
    g_recv,
    gh_full,
    ml_send,
    ml_recv,
    ml_full,
    gl_send,
    gl_sib,
    gl_x,
    t_send,
    t_sib,
    t_all,
    x_sem,
    send_sems,
    mp_sem,
    rs_sem,
    ag_sem,
    fw_sem,
    g_sem,
    gs_sem,
    ml_sem,
    la_sem,
    gls_sem,
    glx_sem,
    ts_sem,
    ta_sem,
):
    pts, var = lax.axis_index("pts"), lax.axis_index("var")
    y, z = lax.div(pts, NZ), lax.rem(pts, NZ)
    x, core = lax.div(var, 2), lax.rem(var, 2)
    other = 1 - core
    sibling = (pts, x * 2 + other)
    chip = pts * NX + x

    def x_peer(d):
        return lax.rem(x + d, NX)

    def send(src, dst, send_sem, recv_sem, device):
        copy = pltpu.make_async_remote_copy(
            src_ref=src,
            dst_ref=dst,
            send_sem=send_sem,
            recv_sem=recv_sem,
            device_id=device,
            device_id_type=MESH,
        )
        copy.start()
        return copy

    def wait_bytes(ref, sem):
        pltpu.make_async_copy(ref, ref, sem).wait()

    loads = [pltpu.make_async_copy(x_hbm.at[k], x_ref.at[k], x_sem.at[k]) for k in range(STEPS)]
    for load in loads:
        load.start()
    barrier = pltpu.get_barrier_semaphore()
    pl.semaphore_signal(barrier, inc=1, device_id=sibling, device_id_type=MESH)

    def chip_device(d):
        target = lax.rem(chip + d, CHIPS)
        return (lax.div(target, NX), lax.rem(target, NX) * 2 + core)

    def greet(d, carry):
        pl.semaphore_signal(barrier, inc=1, device_id=chip_device(d), device_id_type=MESH)
        return carry

    lax.fori_loop(1, CHIPS, greet, 0)

    def pass_levels(k):
        y_ref[k] = lax.dot_general(
            lbf_ref[...], x_ref[k], (((1,), (1,)), ((), ())), preferred_element_type=F32
        )

    def level_gram_start(slot):
        gl_send[...] = packed_gram(lu_ref[...])
        return send(gl_send, gl_sib.at[slot], send_sems.at[0], gls_sem.at[slot], sibling)

    def level_gram_middle(slot, copy):
        copy.wait()
        gl_x[slot, x] = gl_send[...] + gl_sib[slot]
        return [
            send(
                gl_x.at[slot, x],
                gl_x.at[slot, x],
                send_sems.at[d],
                glx_sem.at[slot, d],
                (pts, x_peer(d) * 2 + core),
            )
            for d in range(1, NX)
        ]

    def level_gram_end(slot, copies):
        for copy in copies:
            copy.wait()
        return unpacked(jnp.sum(gl_x[slot], axis=0))

    def column(values, k, lanes):
        return jnp.broadcast_to(values[:, k : k + 1], (values.shape[0], lanes))

    lu_ref[...] = level_ref[...]
    lbf_ref[...] = level_ref[...].astype(BF16)
    tr_ref[...] = time_ref[...]
    tt_ref[...] = lax.dot_general(
        jnp.where(eye_mask(), 1.0, 0.0),
        time_ref[...],
        (((1,), (1,)), ((), ())),
        precision=HIGHEST,
        preferred_element_type=F32,
    )
    slcol_ref[...] = jnp.ones_like(slcol_ref)
    pl.semaphore_wait(barrier, CHIPS)
    first = level_gram_start(0)
    loads[0].wait()
    pass_levels(0)
    second = level_gram_middle(0, first)
    for k in range(1, STEPS):
        loads[k].wait()
        pass_levels(k)
    gl_ref[...] = level_gram_end(0, second)

    share_points = y_ref.shape[2] // (2 * NX)
    quarter = c_ref.shape[2] // NY
    group = RANK // NZ

    def sweep(s, carry):
        time_cols = tt_ref[...]
        weights = time_cols * slcol_ref[...]
        spread = [column(weights, k, share_points) for k in range(STEPS)]

        def point_share(lane_start):
            total = spread[0] * y_ref[0, :, pl.ds(lane_start, share_points)]
            for k in range(1, STEPS):
                total += spread[k] * y_ref[k, :, pl.ds(lane_start, share_points)]
            return total

        def share_lanes(chip_x, c):
            return pl.multiple_of((chip_x * 2 + c) * share_points, share_points)

        for j in range(NX):
            mp_ref[0, j] = point_share(share_lanes(j, other))
        to_sibling = send(mp_ref.at[0], sib_mp.at[s], send_sems.at[0], mp_sem.at[s], sibling)
        for j in range(NX):
            mp_ref[1, j] = point_share(share_lanes(j, core))
        to_sibling.wait()
        for j in range(NX):
            mp_ref[1, j] += sib_mp[s, j]
        scatter = [
            send(
                mp_ref.at[1, x_peer(d)],
                rs_mp.at[s, d - 1],
                send_sems.at[d],
                rs_sem.at[s, d],
                (pts, x_peer(d) * 2 + core),
            )
            for d in range(1, NX)
        ]

        rows = tr_ref[...]
        time_gram = column(time_cols, 0, RANK) * rows[0:1, :]
        for k in range(1, STEPS):
            time_gram += column(time_cols, k, RANK) * rows[k : k + 1, :]
        inverse = ridge_inverse(gl_ref[...] * time_gram)

        for copy in scatter:
            copy.wait()
        own = mp_ref[1, x]
        for d in range(1, NX):
            own += rs_mp[s, d - 1]
        own_lanes = pl.ds(share_lanes(x, core), share_points)
        m_full[s, :, own_lanes] = own
        own_view = m_full.at[s, :, own_lanes]
        gather = [
            send(
                own_view,
                own_view,
                send_sems.at[d],
                ag_sem.at[s, d],
                (pts, x_peer(d) * 2 + core),
            )
            for d in range(1, NX)
        ]
        forward = [send(own_view, own_view, send_sems.at[0], fw_sem.at[s, 0], sibling)]
        for d in (1, 3, 2):
            gather[d - 1].wait()
            source = lax.rem(x + NX - d, NX)
            view = m_full.at[s, :, pl.ds(share_lanes(source, core), share_points)]
            forward.append(send(view, view, send_sems.at[NX + d], fw_sem.at[s, d], sibling))
        for copy in forward:
            copy.wait()

        solved = jnp.dot(inverse, m_full[s], precision=HIGHEST, preferred_element_type=F32)
        pu_ref[...] = solved
        pbf_ref[...] = solved.astype(BF16)

        g_send[...] = packed_gram(solved)
        half = pl.ds(pl.multiple_of(core * 16, 16), 16)
        g_recv[s, pts] = g_send[half, :]

        def pts_device(d):
            return (lax.rem(pts + d, PTS_DEVICES), var)

        for d in range(1, PTS_DEVICES):
            send(
                g_send.at[half, :],
                g_recv.at[s, pts],
                send_sems.at[0],
                g_sem.at[s],
                pts_device(d),
            )

        for dy in (2, 1, 3, 0):
            q = lax.rem(y + dy, NY)
            lanes = pl.ds(pl.multiple_of(q * quarter, quarter), quarter)
            total = None
            for k in range(STEPS):
                product = jnp.dot(pbf_ref[...], x_ref[k, :, lanes], preferred_element_type=F32)
                c_ref[k, :, lanes] = product
                term = column(time_cols, k, quarter) * product
                total = term if total is None else total + term
            for j in range(NZ):
                ml_send[q, j] = total[j * group : (j + 1) * group]
            for dz in (2, 1, 3, 0):
                if dy == 0 and dz == 0:
                    continue
                zz = lax.rem(z + dz, NZ)
                send(
                    ml_send.at[q, zz],
                    ml_recv.at[s, pts],
                    send_sems.at[1],
                    ml_sem.at[s],
                    (q * NZ + zz, var),
                )
        ml_recv[s, pts] = ml_send[y, z]

        others = pl.ds(0, PTS_DEVICES - 1)
        wait_bytes(g_recv.at[s, others], g_sem.at[s])
        wait_bytes(g_recv.at[s, others], send_sems.at[0])
        gh_full[s, half, :] = jnp.sum(g_recv[s], axis=0)
        half_view = gh_full.at[s, half, :]
        half_copy = send(half_view, half_view, send_sems.at[2], gs_sem.at[s], sibling)

        wait_bytes(ml_recv.at[s, others], ml_sem.at[s])
        wait_bytes(ml_recv.at[s, others], send_sems.at[1])
        own_rows = pl.ds(pl.multiple_of(z * group, group), group)
        own_cols = pl.ds(pl.multiple_of(y * quarter, quarter), quarter)
        ml_full[s, own_rows, own_cols] = jnp.sum(ml_recv[s], axis=0)
        level_view = ml_full.at[s, own_rows, own_cols]
        for d in range(1, PTS_DEVICES):
            send(level_view, level_view, send_sems.at[1], la_sem.at[s], pts_device(d))

        half_copy.wait()
        raw_gram = unpacked(gh_full[s])
        point_col, point_row = unit_scales(raw_gram, points_all)
        point_gram = point_col * raw_gram * point_row
        gp_ref[...] = point_gram
        inverse = ridge_inverse(point_gram * time_gram) * point_row
        point_out[...] = pu_ref[...] * point_col

        wait_bytes(ml_recv.at[s, others], la_sem.at[s])
        wait_bytes(ml_recv.at[s, others], send_sems.at[1])
        solved = jnp.dot(inverse, ml_full[s], precision=HIGHEST, preferred_element_type=F32)
        lu_ref[...] = solved
        lbf_ref[...] = solved.astype(BF16)
        scaled = solved * point_col

        lane_ids = lax.broadcasted_iota(jnp.int32, (RANK, 128), 1)
        products = jnp.zeros((RANK, 128), F32)
        for k in range(STEPS):
            sums = jnp.sum(c_ref[k] * scaled, axis=1, keepdims=True)
            products = jnp.where(lane_ids == k, sums, products)
        t_rows = jnp.transpose(products)[:STEPS]
        t_send[:, :RANK] = t_rows
        t_send[:, RANK:] = jnp.zeros_like(t_rows)
        time_copy = send(t_send, t_sib.at[s], send_sems.at[NX], ts_sem.at[s], sibling)
        first = level_gram_start(s + 1)
        time_copy.wait()
        t_all[s, chip] = t_send[...] + t_sib[s]

        def spread_time(d, carry):
            send(
                t_all.at[s, chip],
                t_all.at[s, chip],
                send_sems.at[NX + 1],
                ta_sem.at[s],
                chip_device(d),
            )
            return carry

        lax.fori_loop(1, CHIPS, spread_time, 0)
        second = level_gram_middle(s + 1, first)
        for k in range(STEPS):
            pass_levels(k)
        raw_gram = level_gram_end(s + 1, second)
        level_col, level_row = unit_scales(raw_gram, levels_all)
        level_gram = level_col * raw_gram * level_row
        gl_ref[...] = level_gram
        slcol_ref[...] = jnp.broadcast_to(level_col, slcol_ref.shape)
        inverse = ridge_inverse(gp_ref[...] * level_gram)
        level_out[...] = lu_ref[...] * level_col

        chips = pl.ds(0, CHIPS - 1)
        wait_bytes(t_all.at[s, chips], ta_sem.at[s])
        wait_bytes(t_all.at[s, chips], send_sems.at[NX + 1])
        mttk_time = jnp.sum(t_all[s], axis=0)[:, :RANK] * level_row
        tr_ref[...] = jnp.dot(mttk_time, inverse, precision=HIGHEST, preferred_element_type=F32)
        tt_ref[...] = lax.dot_general(
            inverse,
            mttk_time,
            (((1,), (1,)), ((), ())),
            precision=HIGHEST,
            preferred_element_type=F32,
        )
        return carry

    lax.fori_loop(0, SWEEPS, sweep, 0)
    time_out[...] = tr_ref[...] * math.sqrt(points_all * levels_all)


def solution(mesh):
    def per_device(tensor, level_init, time_init):
        steps, points, levels = tensor.shape
        points_all = points * mesh.shape["pts"]
        levels_all = levels * mesh.shape["var"]
        share = points // (2 * NX)
        group, quarter = RANK // NZ, levels // NY
        vmem = pl.BlockSpec(memory_space=pltpu.VMEM)
        dma = pltpu.SemaphoreType.DMA
        call = pl.pallas_call(
            lambda *refs: sweeps_kernel(points_all, levels_all, *refs),
            out_shape=(
                jax.ShapeDtypeStruct((RANK, points), F32),
                jax.ShapeDtypeStruct((RANK, levels), F32),
                jax.ShapeDtypeStruct((STEPS, RANK), F32),
            ),
            in_specs=[pl.BlockSpec(memory_space=pl.ANY), vmem, vmem],
            out_specs=(vmem, vmem, vmem),
            scratch_shapes=[
                pltpu.VMEM((steps, points, levels), BF16),
                pltpu.VMEM((steps, RANK, points), F32),
                pltpu.VMEM((steps, RANK, levels), F32),
                pltpu.VMEM((RANK, levels), BF16),
                pltpu.VMEM((RANK, points), BF16),
                pltpu.VMEM((RANK, levels), F32),
                pltpu.VMEM((RANK, points), F32),
                pltpu.VMEM((RANK, RANK), F32),
                pltpu.VMEM((RANK, RANK), F32),
                pltpu.VMEM((RANK, STEPS), F32),
                pltpu.VMEM((STEPS, RANK), F32),
                pltpu.VMEM((RANK, STEPS), F32),
                pltpu.VMEM((2, NX, RANK, share), F32),
                pltpu.VMEM((SWEEPS, NX, RANK, share), F32),
                pltpu.VMEM((SWEEPS, NX - 1, RANK, share), F32),
                pltpu.VMEM((SWEEPS, RANK, points), F32),
                pltpu.VMEM((32, 128), F32),
                pltpu.VMEM((SWEEPS, PTS_DEVICES, 16, 128), F32),
                pltpu.VMEM((SWEEPS, 32, 128), F32),
                pltpu.VMEM((NY, NZ, group, quarter), F32),
                pltpu.VMEM((SWEEPS, PTS_DEVICES, group, quarter), F32),
                pltpu.VMEM((SWEEPS, RANK, levels), F32),
                pltpu.VMEM((32, 128), F32),
                pltpu.VMEM((SWEEPS + 1, 32, 128), F32),
                pltpu.VMEM((SWEEPS + 1, NX, 32, 128), F32),
                pltpu.VMEM((8, 128), F32),
                pltpu.VMEM((SWEEPS, 8, 128), F32),
                pltpu.VMEM((SWEEPS, CHIPS, 8, 128), F32),
                dma((STEPS,)),
                dma((2 * NX,)),
                dma((SWEEPS,)),
                dma((SWEEPS, NX)),
                dma((SWEEPS, NX)),
                dma((SWEEPS, NX)),
                dma((SWEEPS,)),
                dma((SWEEPS,)),
                dma((SWEEPS,)),
                dma((SWEEPS,)),
                dma((SWEEPS + 1,)),
                dma((SWEEPS + 1, NX)),
                dma((SWEEPS,)),
                dma((SWEEPS,)),
            ],
            compiler_params=pltpu.CompilerParams(
                collective_id=0, has_side_effects=True, vmem_limit_bytes=48 * 2**20
            ),
            name="als_sweeps",
        )
        return call(tensor, level_init, time_init)

    return jax.shard_map(
        per_device,
        mesh=mesh,
        in_specs=(P(None, "pts", "var"), P(None, "var"), P()),
        out_specs=(P(None, "pts"), P(None, "var"), P()),
        check_vma=False,
    )
```

time: 574 us -> 130 us (0.23); the launches traced: 563 us -> 129 us
  other arithmetic: 142 us -> 0 us
  Pallas kernels: 0 us -> 125 us
  matrix products: 120 us -> 0 us
  waiting for transfers between devices: 110 us -> 0 us
  starting transfers between devices: 83.4 us -> 0 us
  blocking collectives: 58.4 us -> 0 us
  local copies, waits for them, and re-layouts: 28.3 us -> 3.63 us
  between operations: 21.5 us -> 0.65 us
    pallas_call x0 -> x1, Pallas kernels: none -> 125 us  [per_device(): return call(tensor, level_init, time_init)]
    dot_general x58 -> x0, matrix products: 113 us -> none  [the longest x24 58.8 us: per_device(): jnp.einsum('rv,pv->rp', level_bf, tensor[step_index], preferred_element_t...]
    another operation x45 -> x0, other arithmetic: 109 us -> none  [the longest x27 58.7 us: ridge_solve(): chol_lower = jnp.linalg.cholesky(system)]
    all_to_all x20 -> x0, waiting for transfers between devices: 93.4 us -> none  [the longest x17 87.7 us: copy_for_each(): lax.all_to_all(jnp.broadcast_to(array[None], (devices, *array.shape)), ax...]
    all_to_all x20 -> x0, starting transfers between devices: 82.7 us -> none  [the longest x17 71.7 us: copy_for_each(): lax.all_to_all(jnp.broadcast_to(array[None], (devices, *array.shape)), ax...]
    all_to_all x5 -> x0, blocking collectives: 58.4 us -> none  [copy_for_each(): lax.all_to_all(jnp.broadcast_to(array[None], (devices, *array.shape)), ax...]
    all_to_all x19 -> x0, other arithmetic: 18.6 us -> none  [copy_for_each(): lax.all_to_all(jnp.broadcast_to(array[None], (devices, *array.shape)), ax...]
    all_gather x3 -> x0, waiting for transfers between devices: 16.7 us -> none  [total_of_pieces(): return lax.all_gather(array, axis).sum(0)]
  transfers between devices with their start and end apart: 23 -> 0, of which waited for: 23 -> 0; matrix products, arithmetic and copies ran while one was open for 17% -> 0% of each run, Pallas kernels for 0% -> 0%
where the time goes in v1:
time: 130 us; the launch traced here: 129 us
  Pallas kernels  125 us (96%)
  local copies, waits for them, and re-layouts  3.63 us (3%)
    pallas_call x1, Pallas kernels, per_device(): return call(tensor, level_init, time_init)  125 us
    unnamed x7, local copies, waits for them, and re-layouts  3.63 us

profile of v1, /device:TPU:0, one launch (start us, length us, event | category | flops | bytes accessed | tf_op | source)
XLA Modules:
  0.0 129.1 jit_solution(6936126814007326697)
XLA Ops:
  0.6 0.0 copy-start
  0.6 0.9 copy-done
  1.6 0.0 copy-start.1
  1.6 0.7 copy-done.1
  2.3 124.8 %als_sweeps.1 = (f32[64,1024]{1,0:T(8,128)S(1)}, f32[64,1024]{1,0:T(8,128)S(1)}, f32[8,64]{1,0:T(8,128)S(1)}) custom-call(bf16[8,1024,1024]{2,1,0:T(8,128)(2,1)} %refs_0_.1, f32[64,1024]{1,0:T(8,128)S(1)} %copy-done, f32[8,64]{1,0:T(8,128)S(1)} %copy-done.1), custom_call_target="tpu_custom_call" | custom-call | tf_op jit(solution)/shard_map/als_sweeps/pallas_call | solution.py:498
  127.1 0.7 copy.9
  127.8 0.7 copy.10
  128.5 0.6 copy.11
Async XLA Ops:
  0.6 1.0 copy-start
  1.6 0.7 copy-start.1

commit v2 on v1

v2 whole, which is shorter than its diff:
```python
import math

import jax
import jax.numpy as jnp
from jax import lax
from jax.experimental import pallas as pl
from jax.experimental.pallas import tpu as pltpu
from jax.sharding import PartitionSpec as P

RANK = 64
STEPS = 8
SWEEPS = 3
NY = NZ = NX = 4
PTS_DEVICES = NY * NZ
CHIPS = PTS_DEVICES * NX
EPSILON = 1e-06
F32 = jnp.float32
BF16 = jnp.bfloat16
HIGHEST = lax.Precision.HIGHEST
MESH = pl.DeviceIdType.MESH


def inverse_part(tiles, first, last, block=8):
    n = RANK
    shape = (8, n)
    row_ids = lax.broadcasted_iota(jnp.int32, shape, 0)
    lane_ids = lax.broadcasted_iota(jnp.int32, shape, 1)
    for start in range(first, last, block):
        panel = {
            j: [jnp.broadcast_to(tile[:, j : j + 1], shape) for tile in tiles]
            for j in range(start, start + block)
        }
        for k in range(start, start + block):
            t, s = divmod(k, 8)
            inv_pivot = 1.0 / jnp.broadcast_to(panel[k][t][s : s + 1, :], shape)
            col = list(panel[k])
            col[t] = jnp.where(row_ids == s, -1.0, col[t])
            for j in range(k + 1, start + block):
                scaled = jnp.broadcast_to(panel[j][t][s : s + 1, :], shape) * inv_pivot
                new = [panel[j][i] - col[i] * scaled for i in range(n // 8)]
                new[t] = jnp.where(row_ids == s, scaled, new[t])
                panel[j] = new
            row = jnp.broadcast_to(tiles[t][s : s + 1, :], shape) * inv_pivot
            row = jnp.where(lane_ids == k, inv_pivot, row)
            base = [jnp.where(lane_ids == k, 0.0, tile) for tile in tiles]
            base[t] = jnp.where(row_ids == s, 0.0, base[t])
            tiles = [base[i] - col[i] * row for i in range(n // 8)]
    return tiles


def row_tiles(matrix):
    return [matrix[8 * i : 8 * i + 8, :] for i in range(RANK // 8)]


def eye_mask():
    rows = lax.broadcasted_iota(jnp.int32, (RANK, RANK), 0)
    cols = lax.broadcasted_iota(jnp.int32, (RANK, RANK), 1)
    return rows == cols


def ridge_system(gram):
    eye = eye_mask()
    trace = jnp.sum(
        jnp.sum(jnp.where(eye, gram, 0.0), axis=0, keepdims=True), axis=1, keepdims=True
    )
    ridge = 0.01 * trace / RANK + EPSILON
    return gram + jnp.where(eye, ridge, 0.0)


def ridge_inverse(gram):
    return jnp.concatenate(inverse_part(row_tiles(ridge_system(gram)), 0, RANK), axis=0)


def split_gram(factor):
    high = factor.astype(BF16)
    low = (factor - high.astype(F32)).astype(BF16)
    both = jnp.concatenate([high, low], axis=0)
    return lax.dot_general(both, both, (((1,), (1,)), ((), ())), preferred_element_type=F32)


def folded(products):
    rows = products[:RANK] + products[RANK:]
    gram = rows[:, :RANK] + rows[:, RANK:]
    return jnp.concatenate([gram[:32], gram[32:]], axis=1)


def unpacked(packed):
    return jnp.concatenate([packed[:, :RANK], packed[:, RANK:]], axis=0)


def unit_scales(gram, count):
    diag = jnp.where(eye_mask(), gram, 0.0)
    col = 1.0 / jnp.sqrt(jnp.sum(diag, axis=1, keepdims=True) / count + EPSILON)
    row = 1.0 / jnp.sqrt(jnp.sum(diag, axis=0, keepdims=True) / count + EPSILON)
    return col, row


def sweeps_kernel(
    points_all,
    levels_all,
    x_hbm,
    level_hbm,
    time_hbm,
    point_out,
    level_out,
    time_out,
    x_ref,
    y_ref,
    y_sib,
    c_ref,
    lbf_ref,
    lu_ref,
    pu_ref,
    gl_ref,
    gp_ref,
    tt_ref,
    tr_ref,
    tp_ref,
    mp_half,
    sib_mp,
    line,
    m_full,
    g_send,
    g_recv,
    gh_full,
    ml_send,
    ml_recv,
    ml_full,
    inv_ref,
    gl_x,
    t_send,
    t_sib,
    t_all,
    load_sem,
    y_send_sem,
    line_send_sem,
    fw_send_sem,
    gl_send_sem,
    one_send_sem,
    y_sem,
    mp_sem,
    line_sem,
    fw_sem,
    g_sem,
    gs_sem,
    ml_sem,
    la_sem,
    glx_sem,
    ts_sem,
    ta_sem,
):
    pts, var = lax.axis_index("pts"), lax.axis_index("var")
    y, z = lax.div(pts, NZ), lax.rem(pts, NZ)
    x, core = lax.div(var, 2), lax.rem(var, 2)
    other = 1 - core
    sibling = (pts, x * 2 + other)
    chip = pts * NX + x
    xs = [lax.rem(x + d, NX) for d in range(NX)]
    ys = [lax.rem(y + d, NY) for d in range(NY)]
    zs = [lax.rem(z + d, NZ) for d in range(NZ)]
    var_peers = [
        (pts, xs[d] * 2 + c)
        for d, c in (
            (2, other),
            (2, core),
            (1, other),
            (3, other),
            (1, core),
            (3, core),
            (0, other),
        )
    ]
    x_devices = [(pts, xs[d] * 2 + core) for d in range(NX)]
    hops = (0, 1, 2, 1)
    pts_offsets = sorted(
        [(dy, dz) for dy in range(NY) for dz in range(NZ) if dy or dz],
        key=lambda o: -(hops[o[0]] + hops[o[1]]),
    )
    chip_offsets = sorted(
        [(dy, dz, dx) for dy in range(NY) for dz in range(NZ) for dx in range(NX) if dy or dz or dx],
        key=lambda o: -(hops[o[0]] + hops[o[1]] + hops[o[2]]),
    )

    def pts_device(dy, dz):
        return (ys[dy] * NZ + zs[dz], var)

    def chip_device(dy, dz, dx):
        return (ys[dy] * NZ + zs[dz], xs[dx] * 2 + core)

    def send(src, dst, send_sem, recv_sem, device):
        copy = pltpu.make_async_remote_copy(
            src_ref=src,
            dst_ref=dst,
            send_sem=send_sem,
            recv_sem=recv_sem,
            device_id=device,
            device_id_type=MESH,
        )
        copy.start()
        return copy

    def wait_bytes(ref, sem):
        pltpu.make_async_copy(ref, ref, sem).wait()

    level_load = pltpu.make_async_copy(level_hbm, lu_ref, load_sem.at[STEPS])
    time_load = pltpu.make_async_copy(time_hbm, tr_ref, load_sem.at[STEPS + 1])
    loads = [pltpu.make_async_copy(x_hbm.at[k], x_ref.at[k], load_sem.at[k]) for k in range(STEPS)]
    level_load.start()
    time_load.start()
    for load in loads:
        load.start()
    barrier = pltpu.get_barrier_semaphore()
    greeted = [pts_device(*offset) for offset in pts_offsets] + var_peers
    for device in greeted:
        pl.semaphore_signal(barrier, inc=1, device_id=device, device_id_type=MESH)

    half_points = y_ref.shape[3]
    share_points = half_points // NX
    quarter = c_ref.shape[2] // NY
    group = RANK // NZ

    def pass_levels(k):
        product = lax.dot_general(
            lbf_ref[...], x_ref[k], (((1,), (1,)), ((), ())), preferred_element_type=F32
        )
        y_ref[k, 0] = product[:, :half_points]
        y_ref[k, 1] = product[:, half_points:]

    def level_gram_copies(slot):
        view = gl_x.at[slot, var]
        return [
            pltpu.make_async_remote_copy(
                src_ref=view,
                dst_ref=view,
                send_sem=gl_send_sem.at[i],
                recv_sem=glx_sem.at[slot, i],
                device_id=device,
                device_id_type=MESH,
            )
            for i, device in enumerate(var_peers)
        ]

    def level_gram_start(slot, gram):
        gl_x[slot, var] = gram
        for copy in level_gram_copies(slot):
            copy.start()

    def level_gram_end(slot):
        for copy in level_gram_copies(slot):
            copy.wait()
        return unpacked(jnp.sum(gl_x[slot], axis=0))

    def column(values, k, lanes):
        return jnp.broadcast_to(values[:, k : k + 1], (values.shape[0], lanes))

    level_load.wait()
    lbf_ref[...] = lu_ref[...].astype(BF16)
    time_load.wait()
    tt_ref[...] = lax.dot_general(
        jnp.where(eye_mask(), 1.0, 0.0),
        tr_ref[...],
        (((1,), (1,)), ((), ())),
        precision=HIGHEST,
        preferred_element_type=F32,
    )
    for k in range(STEPS):
        loads[k].wait()
        pass_levels(k)
    first_cols = tt_ref[...]

    def first_half(c):
        total = column(first_cols, 0, half_points) * y_ref[0, c]
        for k in range(1, STEPS):
            total += column(first_cols, k, half_points) * y_ref[k, c]
        return total

    mp_half[...] = first_half(other)
    pl.semaphore_wait(barrier, len(greeted))
    to_sibling = send(mp_half, sib_mp, one_send_sem.at[0], mp_sem, sibling)
    level_gram_start(0, folded(split_gram(lu_ref[...])))
    own_half = first_half(core)
    to_sibling.wait()
    own_half += sib_mp[...]
    for j in range(NX):
        line[0, x, j] = own_half[:, j * share_points : (j + 1) * share_points]

    def sweep(s, carry):
        pieces = []
        for j in range(NX):
            view = line.at[s, x, j]
            pieces.append(
                [
                    send(view, view, line_send_sem.at[d, j], line_sem.at[s, d, j], x_devices[d])
                    for d in (2, 1, 3)
                ]
            )

        @pl.when(s == 0)
        def _():
            gl_ref[...] = level_gram_end(0)

        time_cols = tt_ref[...]
        rows = tr_ref[...]
        time_gram = column(time_cols, 0, RANK) * rows[0:1, :]
        for k in range(1, STEPS):
            time_gram += column(time_cols, k, RANK) * rows[k : k + 1, :]
        inverse = ridge_inverse(gl_ref[...] * time_gram)
        inv_ref[...] = inverse

        forward = []

        def arrive(j):
            for copy in pieces[j]:
                copy.wait()
            total = line[s, 0, j]
            for i in range(1, NX):
                total += line[s, i, j]
            m_full[s, j, core] = total
            view = m_full.at[s, j, core]
            forward.append(send(view, view, fw_send_sem.at[j], fw_sem.at[s, j], sibling))

        def solve_points(j):
            forward[j].wait()
            sums = jnp.concatenate([m_full[s, j, 0], m_full[s, j, 1]], axis=1)
            solved = jnp.dot(inverse, sums, precision=HIGHEST, preferred_element_type=F32)
            starts = [c * half_points + j * share_points for c in range(2)]
            for i, start in enumerate(starts):
                pu_ref[:, start : start + share_points] = solved[
                    :, i * share_points : (i + 1) * share_points
                ]
            return solved.astype(BF16), starts

        def block(k, starts, lanes):
            return jnp.concatenate(
                [x_ref[k, start : start + share_points, lanes] for start in starts], axis=0
            )

        arrive(0)
        for j in range(NX - 1):
            arrive(j + 1)
            factor, starts = solve_points(j)
            for k in range(STEPS):
                product = jnp.dot(
                    factor, block(k, starts, slice(None)), preferred_element_type=F32
                )
                c_ref[k] = c_ref[k] + product if j else product
        factor, starts = solve_points(NX - 1)

        spread = [column(time_cols, k, quarter) for k in range(STEPS)]
        for dy in (2, 1, 3, 0):
            q = ys[dy]
            lanes = pl.ds(pl.multiple_of(q * quarter, quarter), quarter)
            total = None
            for k in range(STEPS):
                product = c_ref[k, :, lanes] + jnp.dot(
                    factor, block(k, starts, lanes), preferred_element_type=F32
                )
                c_ref[k, :, lanes] = product
                term = spread[k] * product
                total = term if total is None else total + term
            for j in range(NZ):
                ml_send[q, j] = total[j * group : (j + 1) * group]
            for dz in (2, 1, 3, 0):
                if dy or dz:
                    send(
                        ml_send.at[q, zs[dz]],
                        ml_recv.at[s, pts],
                        one_send_sem.at[1],
                        ml_sem.at[s],
                        pts_device(dy, dz),
                    )
        ml_recv[s, pts] = ml_send[y, z]

        g_send[...] = folded(split_gram(pu_ref[...]))
        half = pl.ds(pl.multiple_of(core * 16, 16), 16)
        g_recv[s, pts] = g_send[half, :]
        for offset in pts_offsets:
            send(
                g_send.at[half, :],
                g_recv.at[s, pts],
                one_send_sem.at[2],
                g_sem.at[s],
                pts_device(*offset),
            )

        others = pl.ds(0, PTS_DEVICES - 1)
        wait_bytes(ml_recv.at[s, others], ml_sem.at[s])
        wait_bytes(ml_recv.at[s, others], one_send_sem.at[1])
        own_rows = pl.ds(pl.multiple_of(z * group, group), group)
        own_cols = pl.ds(pl.multiple_of(y * quarter, quarter), quarter)
        ml_full[s, own_rows, own_cols] = jnp.sum(ml_recv[s], axis=0)
        level_view = ml_full.at[s, own_rows, own_cols]
        for dy, dz in sorted(pts_offsets, key=lambda o: (hops[o[0]], -hops[o[1]])):
            send(
                level_view, level_view, one_send_sem.at[1], la_sem.at[s, dy], pts_device(dy, dz)
            )

        wait_bytes(g_recv.at[s, others], g_sem.at[s])
        wait_bytes(g_recv.at[s, others], one_send_sem.at[2])
        gh_full[s, half, :] = jnp.sum(g_recv[s], axis=0)
        half_view = gh_full.at[s, half, :]
        half_copy = send(half_view, half_view, one_send_sem.at[3], gs_sem.at[s], sibling)
        half_copy.wait()
        raw_gram = unpacked(gh_full[s])
        point_col, point_row = unit_scales(raw_gram, points_all)
        point_gram = point_col * raw_gram * point_row
        gp_ref[...] = point_gram
        inverse = ridge_inverse(point_gram * time_gram) * point_row
        point_out[...] = pu_ref[...] * point_col

        level_products = jnp.zeros((2 * RANK, 2 * RANK), F32)
        for dy in (0, 1, 3, 2):
            count = NZ if dy else NZ - 1
            wait_bytes(ml_recv.at[s, pl.ds(0, count)], la_sem.at[s, dy])
            start = pl.multiple_of(ys[(NY - dy) % NY] * quarter, quarter)
            lanes = pl.ds(start, quarter)
            solved = jnp.dot(
                inverse, ml_full[s, :, lanes], precision=HIGHEST, preferred_element_type=F32
            )
            lu_ref[:, lanes] = solved
            lbf_ref[:, lanes] = solved.astype(BF16)
            level_products += split_gram(solved)
            if dy == 2:
                level_gram_start(s + 1, folded(level_products))
            scaled = solved * point_col
            for k in range(STEPS):
                product = c_ref[k, :, lanes] * scaled
                part = product[:, :128]
                for i in range(128, quarter, 128):
                    part += product[:, i : i + 128]
                tp_ref[k] = tp_ref[k] + part if dy else part
        lane_ids = lax.broadcasted_iota(jnp.int32, (RANK, 128), 1)
        products = jnp.zeros((RANK, 128), F32)
        for k in range(STEPS):
            sums = jnp.sum(tp_ref[k], axis=1, keepdims=True)
            products = jnp.where(lane_ids == k, sums, products)
        t_rows = jnp.transpose(products)[:STEPS]
        t_send[...] = jnp.concatenate([t_rows[:4], t_rows[4:]], axis=1)
        time_copy = send(t_send, t_sib.at[s], one_send_sem.at[4], ts_sem.at[s], sibling)
        wait_bytes(ml_recv.at[s, others], one_send_sem.at[1])
        time_copy.wait()
        t_all[s, chip] = t_send[...] + t_sib[s]
        time_view = t_all.at[s, chip]
        for offset in chip_offsets:
            send(time_view, time_view, one_send_sem.at[5], ta_sem.at[s], chip_device(*offset))

        y_copies = []

        def next_products(first, last):
            for k in range(first, last):
                pass_levels(k)
            for k in range(first, last):
                half_view = y_ref.at[k, other]
                y_copies.append(
                    send(half_view, y_sib.at[s, k], y_send_sem.at[k], y_sem.at[s, k], sibling)
                )

        next_products(0, 2)
        next_products(2, 4)
        raw_gram = level_gram_end(s + 1)
        level_col, level_row = unit_scales(raw_gram, levels_all)
        level_gram = level_col * raw_gram * level_row
        gl_ref[...] = level_gram
        tiles = inverse_part(row_tiles(ridge_system(gp_ref[...] * level_gram)), 0, RANK // 2)
        inv_ref[...] = jnp.concatenate(tiles, axis=0)
        next_products(4, 6)
        tiles = inverse_part(row_tiles(inv_ref[...]), RANK // 2, RANK)
        inverse = jnp.concatenate(tiles, axis=0)
        inv_ref[...] = inverse
        level_out[...] = lu_ref[...] * level_col
        next_products(6, 8)
        chips = pl.ds(0, CHIPS - 1)
        wait_bytes(t_all.at[s, chips], ta_sem.at[s])
        wait_bytes(t_all.at[s, chips], one_send_sem.at[5])
        mttk_time = unpacked(jnp.sum(t_all[s], axis=0)) * level_row
        tr_ref[...] = jnp.dot(mttk_time, inverse, precision=HIGHEST, preferred_element_type=F32)
        next_cols = lax.dot_general(
            inverse,
            mttk_time,
            (((1,), (1,)), ((), ())),
            precision=HIGHEST,
            preferred_element_type=F32,
        )
        tt_ref[...] = next_cols
        for copy in y_copies:
            copy.wait()

        @pl.when(s < SWEEPS - 1)
        def _():
            weights = next_cols * level_col
            for j in range(NX):
                lanes = slice(j * share_points, (j + 1) * share_points)
                total = None
                for k in range(STEPS):
                    both = y_ref[k, core, :, lanes] + y_sib[s, k, :, lanes]
                    term = column(weights, k, share_points) * both
                    total = term if total is None else total + term
                line[s + 1, x, j] = total

        return carry

    lax.fori_loop(0, SWEEPS, sweep, 0)
    time_out[...] = tr_ref[...] * math.sqrt(points_all * levels_all)


def hand_over(point_in, level_in, time_in, point_out, level_out, time_out):
    point_out[...] = point_in[...]
    level_out[...] = level_in[...]
    time_out[...] = time_in[...]


def solution(mesh):
    def per_device(tensor, level_init, time_init):
        steps, points, levels = tensor.shape
        points_all = points * mesh.shape["pts"]
        levels_all = levels * mesh.shape["var"]
        share = points // (2 * NX)
        group, quarter = RANK // NZ, levels // NY
        anywhere = pl.BlockSpec(memory_space=pl.ANY)
        vmem = pl.BlockSpec(memory_space=pltpu.VMEM)
        dma = pltpu.SemaphoreType.DMA
        outputs = (
            jax.ShapeDtypeStruct((RANK, points), F32),
            jax.ShapeDtypeStruct((RANK, levels), F32),
            jax.ShapeDtypeStruct((STEPS, RANK), F32),
        )
        call = pl.pallas_call(
            lambda *refs: sweeps_kernel(points_all, levels_all, *refs),
            out_shape=outputs,
            in_specs=[anywhere, anywhere, anywhere],
            out_specs=(vmem, vmem, vmem),
            scratch_shapes=[
                pltpu.VMEM((steps, points, levels), BF16),
                pltpu.VMEM((steps, 2, RANK, points // 2), F32),
                pltpu.VMEM((SWEEPS, steps, RANK, points // 2), F32),
                pltpu.VMEM((steps, RANK, levels), F32),
                pltpu.VMEM((RANK, levels), BF16),
                pltpu.VMEM((RANK, levels), F32),
                pltpu.VMEM((RANK, points), F32),
                pltpu.VMEM((RANK, RANK), F32),
                pltpu.VMEM((RANK, RANK), F32),
                pltpu.VMEM((RANK, STEPS), F32),
                pltpu.VMEM((STEPS, RANK), F32),
                pltpu.VMEM((STEPS, RANK, 128), F32),
                pltpu.VMEM((RANK, points // 2), F32),
                pltpu.VMEM((RANK, points // 2), F32),
                pltpu.VMEM((SWEEPS, NX, NX, RANK, share), F32),
                pltpu.VMEM((SWEEPS, NX, 2, RANK, share), F32),
                pltpu.VMEM((32, 128), F32),
                pltpu.VMEM((SWEEPS, PTS_DEVICES, 16, 128), F32),
                pltpu.VMEM((SWEEPS, 32, 128), F32),
                pltpu.VMEM((NY, NZ, group, quarter), F32),
                pltpu.VMEM((SWEEPS, PTS_DEVICES, group, quarter), F32),
                pltpu.VMEM((SWEEPS, RANK, levels), F32),
                pltpu.VMEM((RANK, RANK), F32),
                pltpu.VMEM((SWEEPS + 1, 2 * NX, 32, 128), F32),
                pltpu.VMEM((4, 128), F32),
                pltpu.VMEM((SWEEPS, 4, 128), F32),
                pltpu.VMEM((SWEEPS, CHIPS, 4, 128), F32),
                dma((STEPS + 2,)),
                dma((STEPS,)),
                dma((NX, NX)),
                dma((NX,)),
                dma((2 * NX - 1,)),
                dma((6,)),
                dma((SWEEPS, STEPS)),
                dma,
                dma((SWEEPS, NX, NX)),
                dma((SWEEPS, NX)),
                dma((SWEEPS,)),
                dma((SWEEPS,)),
                dma((SWEEPS,)),
                dma((SWEEPS, NY)),
                dma((SWEEPS + 1, 2 * NX - 1)),
                dma((SWEEPS,)),
                dma((SWEEPS,)),
            ],
            compiler_params=pltpu.CompilerParams(
                collective_id=0, has_side_effects=True, vmem_limit_bytes=63 * 2**20
            ),
            name="als_sweeps",
        )
        results = call(tensor, level_init, time_init)
        return pl.pallas_call(
            hand_over,
            out_shape=outputs,
            in_specs=[vmem, vmem, vmem],
            out_specs=(vmem, vmem, vmem),
            name="hand_over",
        )(*results)

    return jax.shard_map(
        per_device,
        mesh=mesh,
        in_specs=(P(None, "pts", "var"), P(None, "var"), P()),
        out_specs=(P(None, "pts"), P(None, "var"), P()),
        check_vma=False,
    )
```

time: 130 us -> 118 us (0.908)
  Pallas kernels: 125 us -> 116 us
  local copies, waits for them, and re-layouts: 3.63 us -> 0 us
    pallas_call x1 -> x2, Pallas kernels: 125 us -> 116 us  [the longest x1 114 us: per_device(): results = call(tensor, level_init, time_init)]
    unnamed x7 -> x0, local copies, waits for them, and re-layouts: 3.63 us -> none
where the time goes in v2:
time: 118 us; the launch traced here: 116 us
  Pallas kernels  116 us (98%)
    pallas_call x1, Pallas kernels, per_device(): results = call(tensor, level_init, time_init)  114 us

profile of v2, /device:TPU:0, one launch (start us, length us, event | category | flops | bytes accessed | tf_op | source)
XLA Modules:
  0.0 116.3 jit_solution(1494787490176313277)
XLA Ops:
  0.6 113.8 %als_sweeps.1 = (f32[64,1024]{1,0:T(8,128)}, f32[64,1024]{1,0:T(8,128)}, f32[8,64]{1,0:T(8,128)}) custom-call(bf16[8,1024,1024]{2,1,0:T(8,128)(2,1)} %refs_0_.1, f32[64,1024]{1,0:T(8,128)} %refs_1_.1, f32[8,64]{1,0:T(8,128)} %refs_2_.1), custom_call_target="tpu_custom_call" | custom-call | tf_op jit(solution)/shard_map/als_sweeps/pallas_call | solution.py:583
  114.5 1.8 %hand_over.1 = (f32[64,1024]{1,0:T(8,128)}, f32[64,1024]{1,0:T(8,128)}, f32[8,64]{1,0:T(8,128)}) custom-call(f32[64,1024]{1,0:T(8,128)} %get-tuple-element.6.point_in, f32[64,1024]{1,0:T(8,128)} %get-tuple-element.7.level_in, f32[8,64]{1,0:T(8,128)} %get-tuple-element.8.time_in), custom_call_target="tpu_custom_call" | custom-call | tf_op jit(solution)/shard_map/hand_over/pallas_call | solution.py:584

commit v3 on v2

--- a/solution.py
+++ b/solution.py
@@ -202,6 +202,10 @@
     def wait_bytes(ref, sem):
         pltpu.make_async_copy(ref, ref, sem).wait()
 
+    barrier = pltpu.get_barrier_semaphore()
+    greeted = [pts_device(*offset) for offset in pts_offsets] + var_peers
+    for device in greeted:
+        pl.semaphore_signal(barrier, inc=1, device_id=device, device_id_type=MESH)
     level_load = pltpu.make_async_copy(level_hbm, lu_ref, load_sem.at[STEPS])
     time_load = pltpu.make_async_copy(time_hbm, tr_ref, load_sem.at[STEPS + 1])
     loads = [pltpu.make_async_copy(x_hbm.at[k], x_ref.at[k], load_sem.at[k]) for k in range(STEPS)]
@@ -209,10 +213,6 @@
     time_load.start()
     for load in loads:
         load.start()
-    barrier = pltpu.get_barrier_semaphore()
-    greeted = [pts_device(*offset) for offset in pts_offsets] + var_peers
-    for device in greeted:
-        pl.semaphore_signal(barrier, inc=1, device_id=device, device_id_type=MESH)
 
     half_points = y_ref.shape[3]
     share_points = half_points // NX
@@ -252,6 +252,20 @@
 
     def column(values, k, lanes):
         return jnp.broadcast_to(values[:, k : k + 1], (values.shape[0], lanes))
+
+    def piece_copies(s, j):
+        view = line.at[s, x, j]
+        return [
+            pltpu.make_async_remote_copy(
+                src_ref=view,
+                dst_ref=view,
+                send_sem=line_send_sem.at[d, j],
+                recv_sem=line_sem.at[s, d, j],
+                device_id=x_devices[d],
+                device_id_type=MESH,
+            )
+            for d in (2, 1, 3)
+        ]
 
     level_load.wait()
     lbf_ref[...] = lu_ref[...].astype(BF16)
@@ -283,17 +297,11 @@
     own_half += sib_mp[...]
     for j in range(NX):
         line[0, x, j] = own_half[:, j * share_points : (j + 1) * share_points]
+        for copy in piece_copies(0, j):
+            copy.start()
 
     def sweep(s, carry):
-        pieces = []
-        for j in range(NX):
-            view = line.at[s, x, j]
-            pieces.append(
-                [
-                    send(view, view, line_send_sem.at[d, j], line_sem.at[s, d, j], x_devices[d])
-                    for d in (2, 1, 3)
-                ]
-            )
+        pieces = [piece_copies(s, j) for j in range(NX)]
 
         @pl.when(s == 0)
         def _():
@@ -385,11 +393,11 @@
 
         others = pl.ds(0, PTS_DEVICES - 1)
         wait_bytes(ml_recv.at[s, others], ml_sem.at[s])
-        wait_bytes(ml_recv.at[s, others], one_send_sem.at[1])
         own_rows = pl.ds(pl.multiple_of(z * group, group), group)
         own_cols = pl.ds(pl.multiple_of(y * quarter, quarter), quarter)
         ml_full[s, own_rows, own_cols] = jnp.sum(ml_recv[s], axis=0)
         level_view = ml_full.at[s, own_rows, own_cols]
+        wait_bytes(ml_recv.at[s, others], one_send_sem.at[1])
         for dy, dz in sorted(pts_offsets, key=lambda o: (hops[o[0]], -hops[o[1]])):
             send(
                 level_view, level_view, one_send_sem.at[1], la_sem.at[s, dy], pts_device(dy, dz)
@@ -496,6 +504,8 @@
                     term = column(weights, k, share_points) * both
                     total = term if total is None else total + term
                 line[s + 1, x, j] = total
+                for copy in piece_copies(s + 1, j):
+                    copy.start()
 
         return carry
 

time: 118 us -> 118 us (level)
  no operation moved by 1% of the time
where the time goes in v3:
time: 118 us; the launch traced here: 117 us
  Pallas kernels  116 us (98%)
    pallas_call x1, Pallas kernels, per_device(): results = call(tensor, level_init, time_init)  115 us

profile of v3, /device:TPU:0, one launch (start us, length us, event | category | flops | bytes accessed | tf_op | source)
XLA Modules:
  0.0 117.1 jit_solution(11378030016897674963)
XLA Ops:
  0.6 114.6 %als_sweeps.1 = (f32[64,1024]{1,0:T(8,128)}, f32[64,1024]{1,0:T(8,128)}, f32[8,64]{1,0:T(8,128)}) custom-call(bf16[8,1024,1024]{2,1,0:T(8,128)(2,1)} %refs_0_.1, f32[64,1024]{1,0:T(8,128)} %refs_1_.1, f32[8,64]{1,0:T(8,128)} %refs_2_.1), custom_call_target="tpu_custom_call" | custom-call | tf_op jit(solution)/shard_map/als_sweeps/pallas_call | solution.py:593
  115.2 1.8 %hand_over.1 = (f32[64,1024]{1,0:T(8,128)}, f32[64,1024]{1,0:T(8,128)}, f32[8,64]{1,0:T(8,128)}) custom-call(f32[64,1024]{1,0:T(8,128)} %get-tuple-element.6.point_in, f32[64,1024]{1,0:T(8,128)} %get-tuple-element.7.level_in, f32[8,64]{1,0:T(8,128)} %get-tuple-element.8.time_in), custom_call_target="tpu_custom_call" | custom-call | tf_op jit(solution)/shard_map/hand_over/pallas_call | solution.py:594
